TPU v7x, 32 devices: a whole 2x2x4 slice. The times are simulated.
32 devices in a mesh: groups: 2 (over x), seq: 8 (over z, y), mp: 2 (over core).
Axes of the slice: x: 2, y: 2, z: 4, core: 2. Of those that a mesh axis runs over, the one named last changes fastest.
Arguments:
- queries: bfloat16 [8192, 4096], P(('groups', 'seq'), 'mp'), parts along dimension 0, may hold values from -6 to 6
- keys: bfloat16 [8192, 512], P(('groups', 'seq'), 'mp'), parts along dimension 0, may hold values from -6 to 6
- values: bfloat16 [8192, 512], P(('groups', 'seq'), 'mp'), parts along dimension 0, may hold values from -6 to 6
- feat_weight: bfloat16 [32, 128, 128], P('mp'), may hold values from -0.5 to 0.5
- head_gain: float32 [4096], P('mp'), may hold values from 0.1 to 1.9
- out_weight: bfloat16 [4096, 4096], P('mp'), may hold values from -0.09375 to 0.09375
Outputs:
- mixed: bfloat16 [8192, 4096], P(('groups', 'seq', 'mp')), parts along dimension 0
There are 2 independent parts, one for each index of `groups`. A program takes and returns all parts, laid end to end along the dimension named above; an argument that names none is the same for every part. Nothing has to cross between parts.
All inputs are finite; a program needn't handle non-finite values.
Results may differ from a plain program's by a relative error of at most 0.0083.
Values sent between devices are 32-bit elements; how exact they have to be, the bound alone decides.
A program may use at most 128 MiB of HBM per device.

v0:
```python
import functools

import jax
import jax.numpy as jnp
from jax import lax
from jax.experimental import pallas as pl
from jax.experimental.pallas import tpu as pltpu
from jax.sharding import PartitionSpec as P

HD = 128
PAIR = 2 * HD
COLS = 512
MESH = pl.DeviceIdType.MESH
NT = (((1,), (1,)), ((), ()))


def feature(mapped):
    return jnp.where(mapped > 0.0, mapped + 1.0, jnp.exp(jnp.minimum(mapped, 0.0))).astype(jnp.bfloat16)


def kernel(
    n_seq, q_hbm, k_hbm, v_hbm, fw_hbm, gain_hbm, w_hbm, out_ref,
    q_buf, k_buf, v_buf, fw_buf, gain_buf, w_buf,
    vt_buf, fk_buf, fq_buf, intra_buf, nrm_buf, acc,
    s_buf, peer_s, p_buf, fwd, pre_out, pre_in, mp_recv,
    q_sem, kv_sem, w_sem,
    y_send, y_recv, z_send, z_recv, b_send, b_recv, mp_send, mp_recv_sem,
):
    grp = lax.axis_index("groups")
    me = lax.axis_index("seq")
    mp = lax.axis_index("mp")
    layer = lax.div(me, 2)
    side = lax.rem(me, 2)
    mate = (grp, me + 1 - 2 * side, mp)
    up = (grp, me + 2, mp)
    down = (grp, me - 2, mp)
    other_mp = 1 - mp
    peer = (grp, me, other_mp)
    has_down = layer > 0
    has_up = me + 2 < n_seq
    n_pairs = q_buf.shape[0]
    rows = q_buf.shape[1]
    half = rows // 2
    n_cols = acc.shape[0]
    n_kv = k_buf.shape[1] // HD
    pairs_kv = n_pairs // n_kv
    own_pairs = n_pairs // 2
    own_heads = 2 * own_pairs
    own_at = side * own_pairs
    mate_at = own_pairs - own_at

    def k_copy():
        return pltpu.make_async_copy(k_hbm, k_buf, kv_sem.at[0])

    def v_copy():
        return pltpu.make_async_copy(v_hbm, v_buf, kv_sem.at[1])

    def fw_copy():
        return pltpu.make_async_copy(fw_hbm, fw_buf, kv_sem.at[2])

    def gain_copy():
        return pltpu.make_async_copy(gain_hbm, gain_buf, kv_sem.at[3])

    def q_copy(i):
        at = pl.multiple_of(i * PAIR, PAIR)
        return pltpu.make_async_copy(q_hbm.at[:, pl.ds(at, PAIR)], q_buf.at[i], q_sem.at[i])

    def w_copy(i):
        at = pl.multiple_of(i * PAIR, PAIR)
        return pltpu.make_async_copy(w_hbm.at[pl.ds(at, PAIR), :], w_buf.at[lax.div(i, own_pairs), pl.ds(pl.multiple_of(lax.rem(i, own_pairs) * PAIR, PAIR), PAIR)], w_sem.at[i])

    def y_copy(i):
        return pltpu.make_async_remote_copy(
            src_ref=s_buf.at[2 * mate_at + i], dst_ref=peer_s.at[i], send_sem=y_send.at[i],
            recv_sem=y_recv.at[i], device_id=mate, device_id_type=MESH)

    def z_copy(i):
        return pltpu.make_async_remote_copy(
            src_ref=fwd.at[i], dst_ref=p_buf.at[i], send_sem=z_send.at[i],
            recv_sem=z_recv.at[i], device_id=up, device_id_type=MESH)

    def b_copy(i):
        return pltpu.make_async_remote_copy(
            src_ref=pre_out.at[i], dst_ref=pre_in.at[i], send_sem=b_send.at[i],
            recv_sem=b_recv.at[i], device_id=mate, device_id_type=MESH)

    def mp_copy(c):
        return pltpu.make_async_remote_copy(
            src_ref=acc.at[c, pl.ds(pl.multiple_of(other_mp * half, half), half)],
            dst_ref=mp_recv.at[c], send_sem=mp_send.at[c],
            recv_sem=mp_recv_sem.at[c], device_id=peer, device_id_type=MESH)

    k_copy().start()
    fw_copy().start()
    v_copy().start()
    gain_copy().start()

    @pl.loop(0, n_pairs)
    def _(i):
        q_copy(i).start()

    @pl.loop(0, n_pairs)
    def _(i):
        w_copy(i).start()

    barrier = pltpu.get_barrier_semaphore()
    pl.semaphore_signal(barrier, inc=1, device_id=mate, device_id_type=MESH)
    pl.semaphore_signal(barrier, inc=1, device_id=peer, device_id_type=MESH)

    @pl.when(has_up)
    def _():
        pl.semaphore_signal(barrier, inc=1, device_id=up, device_id_type=MESH)

    @pl.when(has_down)
    def _():
        pl.semaphore_signal(barrier, inc=1, device_id=down, device_id_type=MESH)

    pl.semaphore_wait(barrier, 2 + has_up.astype(jnp.int32) + has_down.astype(jnp.int32))

    @pl.when(jnp.logical_not(has_down))
    def _():
        p_buf[...] = jnp.zeros_like(p_buf)

    k_copy().wait()
    fw_copy().wait()
    v_copy().wait()

    def states(i):
        kv_at = pl.multiple_of(lax.div(i, pairs_kv) * HD, HD)
        weight = jnp.concatenate([fw_buf[2 * i], fw_buf[2 * i + 1]], axis=1)
        fk = feature(jnp.dot(k_buf[:, pl.ds(kv_at, HD)], weight, preferred_element_type=jnp.float32))
        fk_buf[i] = fk
        state = jnp.dot(vt_buf[lax.div(i, pairs_kv)], fk, preferred_element_type=jnp.float32)
        s_buf[2 * i] = state[:, :HD]
        s_buf[2 * i + 1] = state[:, HD:]

    for g in range(n_kv):
        vt_buf[g] = v_buf[:, g * HD:(g + 1) * HD].T

    @pl.loop(0, own_pairs)
    def _(t):
        states(mate_at + t)
        y_copy(2 * t).start()
        y_copy(2 * t + 1).start()

    @pl.loop(0, own_pairs)
    def _(t):
        states(own_at + t)

    gain_copy().wait()

    def intra(i):
        q_copy(i).wait()
        zero = jnp.zeros((HD, HD), jnp.bfloat16)
        weight = jnp.concatenate(
            [jnp.concatenate([fw_buf[2 * i], zero], axis=1),
             jnp.concatenate([zero, fw_buf[2 * i + 1]], axis=1)], axis=0)
        fq = feature(jnp.dot(q_buf[i], weight, preferred_element_type=jnp.float32))
        fq_buf[i] = fq
        kv_at = pl.multiple_of(lax.div(i, pairs_kv) * HD, HD)
        values = v_buf[:, pl.ds(kv_at, HD)]
        causal = (lax.broadcasted_iota(jnp.int32, (half, half), 0)
                  >= lax.broadcasted_iota(jnp.int32, (half, half), 1))
        for j in range(2):
            lanes = slice(j * HD, (j + 1) * HD)
            fk_h = fk_buf[i, :, lanes]
            fq_h = fq[:, lanes]
            top = lax.dot_general(fq_h[:half], fk_h[:half], NT, preferred_element_type=jnp.float32)
            top = jnp.where(causal, top, 0.0).astype(jnp.bfloat16)
            intra_buf[i, :half, lanes] = jnp.dot(top, values[:half], preferred_element_type=jnp.float32)
            left = lax.dot_general(fq_h[half:], fk_h[:half], NT, preferred_element_type=jnp.float32)
            right = lax.dot_general(fq_h[half:], fk_h[half:], NT, preferred_element_type=jnp.float32)
            right = jnp.where(causal, right, 0.0)
            low = jnp.concatenate([left.astype(jnp.bfloat16), right.astype(jnp.bfloat16)], axis=1)
            intra_buf[i, half:, lanes] = jnp.dot(low, values, preferred_element_type=jnp.float32)

    def serve(k):
        y_copy(k).wait_recv()

        @pl.when(has_down)
        def _():
            z_copy(k).wait_recv()

        @pl.when(has_up)
        def _():
            fwd[k] = p_buf[k] + s_buf[2 * own_at + k] + peer_s[k]
            z_copy(k).start()

        pre_out[k] = p_buf[k] + jnp.where(side == 0, s_buf[2 * own_at + k], 0.0)
        b_copy(k).start()

    def finish(i, grp_at, prefixes):
        for j in range(2):
            lanes = slice(j * HD, (j + 1) * HD)
            high = prefixes[j].astype(jnp.bfloat16)
            low = (prefixes[j] - high.astype(jnp.float32)).astype(jnp.bfloat16)
            fq_h = fq_buf[i, :, lanes]
            inter = lax.dot_general(
                jnp.concatenate([fq_h, fq_h], axis=1),
                jnp.concatenate([high, low], axis=1),
                NT, preferred_element_type=jnp.float32)
            attn = inter + intra_buf[i, :, lanes]
            scale = lax.rsqrt(jnp.mean(attn * attn, axis=-1, keepdims=True) + 1e-06)
            gain = gain_buf[pl.ds(2 * i + j, 1), :]
            at = pl.multiple_of(lax.rem(i, own_pairs) * PAIR + j * HD, HD)
            nrm_buf[grp_at, :, pl.ds(at, HD)] = (attn * scale * gain).astype(jnp.bfloat16)

    def finish_own(m):
        finish(own_at + m, side, [
            p_buf[2 * m + j] + jnp.where(side == 1, peer_s[2 * m + j], 0.0) for j in range(2)])

    def finish_mate(m):
        b_copy(2 * m).wait_recv()
        b_copy(2 * m + 1).wait_recv()
        finish(mate_at + m, 1 - side, [pre_in[2 * m], pre_in[2 * m + 1]])

    @pl.loop(0, own_heads + n_seq // 2 - 1)
    def _(t):
        @pl.when(t < n_pairs)
        def _():
            intra(lax.rem(own_at + t, n_pairs))

        k = t - layer

        @pl.when(jnp.logical_and(k >= 0, k < own_heads))
        def _():
            serve(k)

            @pl.when(lax.rem(k, 2) == 1)
            def _():
                finish_own(lax.div(k, 2))

    @pl.loop(0, n_pairs)
    def _(i):
        w_copy(i).wait()

    cols_each = n_cols // own_pairs

    @pl.loop(0, own_pairs)
    def _(m):
        @pl.loop(m * cols_each, (m + 1) * cols_each)
        def _(c):
            at = pl.multiple_of(c * COLS, COLS)
            acc[c] = jnp.dot(nrm_buf[side], w_buf[side, :, pl.ds(at, COLS)], preferred_element_type=jnp.float32)

        finish_mate(m)

    theirs = pl.ds(pl.multiple_of(other_mp * half, half), half)
    mine = pl.ds(pl.multiple_of(mp * half, half), half)
    rest = 1 - side

    @pl.loop(0, n_cols)
    def _(c):
        at = pl.multiple_of(c * COLS, COLS)
        acc[c, theirs] += jnp.dot(nrm_buf[rest, theirs], w_buf[rest, :, pl.ds(at, COLS)], preferred_element_type=jnp.float32)
        mp_copy(c).start()

    @pl.loop(0, n_cols)
    def _(c):
        at = pl.multiple_of(c * COLS, COLS)
        total = acc[c, mine] + jnp.dot(nrm_buf[rest, mine], w_buf[rest, :, pl.ds(at, COLS)], preferred_element_type=jnp.float32)
        mp_copy(c).wait_recv()
        out_ref[:, pl.ds(at, COLS)] = (total + mp_recv[c]).astype(jnp.bfloat16)

    @pl.loop(0, own_heads)
    def _(i):
        y_copy(i).wait_send()
        b_copy(i).wait_send()

        @pl.when(has_up)
        def _():
            z_copy(i).wait_send()

    @pl.loop(0, n_cols)
    def _(c):
        mp_copy(c).wait_send()


def body(n_seq, queries, keys, values, feat_weight, head_gain, out_weight):
    rows, feats = queries.shape
    heads = feat_weight.shape[0]
    n_pairs = heads // 2
    dout = out_weight.shape[1]
    n_cols = dout // COLS
    half = rows // 2
    bf, f32 = jnp.bfloat16, jnp.float32
    gain = head_gain.reshape(heads, HD)
    dma = pltpu.SemaphoreType.DMA
    return pl.pallas_call(
        functools.partial(kernel, n_seq),
        out_shape=pltpu.VMEM((half, dout), bf),
        in_specs=[pl.BlockSpec(memory_space=pl.ANY)] * 6,
        out_specs=pl.BlockSpec(memory_space=pltpu.VMEM),
        scratch_shapes=[
            pltpu.VMEM((n_pairs, rows, PAIR), bf),
            pltpu.VMEM(keys.shape, bf),
            pltpu.VMEM(values.shape, bf),
            pltpu.VMEM(feat_weight.shape, bf),
            pltpu.VMEM((heads, HD), f32),
            pltpu.VMEM((2, feats // 2, dout), bf),
            pltpu.VMEM((keys.shape[1] // HD, HD, rows), bf),
            pltpu.VMEM((n_pairs, rows, PAIR), bf),
            pltpu.VMEM((n_pairs, rows, PAIR), bf),
            pltpu.VMEM((n_pairs, rows, PAIR), f32),
            pltpu.VMEM((2, rows, feats // 2), bf),
            pltpu.VMEM((n_cols, rows, COLS), f32),
            pltpu.VMEM((heads, HD, HD), f32),
            pltpu.VMEM((n_pairs, HD, HD), f32),
            pltpu.VMEM((n_pairs, HD, HD), f32),
            pltpu.VMEM((n_pairs, HD, HD), f32),
            pltpu.VMEM((n_pairs, HD, HD), f32),
            pltpu.VMEM((n_pairs, HD, HD), f32),
            pltpu.VMEM((n_cols, half, COLS), f32),
            dma((n_pairs,)), dma((4,)), dma((n_pairs,)),
            dma((n_pairs,)), dma((n_pairs,)), dma((n_pairs,)), dma((n_pairs,)),
            dma((n_pairs,)), dma((n_pairs,)),
            dma((n_cols,)), dma((n_cols,)),
        ],
        compiler_params=pltpu.CompilerParams(
            collective_id=0, has_side_effects=True, vmem_limit_bytes=58 * 1024 * 1024),
        cost_estimate=pl.CostEstimate(
            flops=2 * rows * feats * dout, bytes_accessed=feats * dout * 2, transcendentals=0),
    )(queries, keys, values, feat_weight, gain, out_weight)


def solution(mesh):
    return jax.shard_map(
        functools.partial(body, mesh.shape["seq"]),
        mesh=mesh,
        in_specs=(
            P(("groups", "seq"), "mp"),
            P(("groups", "seq"), "mp"),
            P(("groups", "seq"), "mp"),
            P("mp", None, None),
            P("mp"),
            P("mp", None),
        ),
        out_specs=P(("groups", "seq", "mp"), None),
        check_vma=False,
    )
```

profile of v0, /device:TPU:26, one launch (start us, length us, event | category | flops | bytes accessed | tf_op | source)
XLA Modules:
  0.0 42.3 jit_solution(16949661562389545639)
XLA Ops:
  0.0 41.0 %shard_map.64 = bf16[256,4096]{1,0:T(8,128)(2,1)S(1)} custom-call(bf16[512,2048]{1,0:T(8,128)(2,1)} %q_hbm.1, bf16[512,256]{1,0:T(8,128)(2,1)} %k_hbm.1, bf16[512,256]{1,0:T(8,128)(2,1)} %v_hbm.1, bf16[16,128,128]{2,1,0:T(8,128)(2,1)} %fw_hbm.1, f32[16,128]{1,0:T(8,128)} %bitcast.1, bf16[2048,4096]{1,0:T(8,128)(2,1)} %w_hbm.1), custom_call_target="tpu_custom_call" | custom-call | flops 8589934592 | bytes 16777216 | tf_op jit(solution)/shard_map/pallas_call | solution.py:289
  41.0 1.3 %copy.8 = bf16[256,4096]{1,0:T(8,128)(2,1)} copy(bf16[256,4096]{1,0:T(8,128)(2,1)S(1)} %shard_map.64) | data formatting | bytes 4194304
where the time goes:
time: 42.8 us; the launch traced here: 42.3 us
  Pallas kernels  41 us (96%)
  local copies, waits for them, and re-layouts  1.32 us (3%)
    pallas_call x1, Pallas kernels, body(): pl.pallas_call(functools.partial(kernel, n_seq), out_shape=pltpu.VMEM((ha...  41 us
    unnamed x1, local copies, waits for them, and re-layouts  1.32 us

commit v1 on v0

v1 whole, which is shorter than its diff:
```python
import functools

import jax
import jax.numpy as jnp
from jax import lax
from jax.experimental import pallas as pl
from jax.experimental.pallas import tpu as pltpu
from jax.sharding import PartitionSpec as P

HD = 128
PAIR = 2 * HD
COLS = 512
CUTS = 1
TAIL = 2
AHEAD = 2
MORE = 2
PART = HD // CUTS
MESH = pl.DeviceIdType.MESH
NT = (((1,), (1,)), ((), ()))


def feature(mapped):
    return jnp.where(mapped > 0.0, mapped + 1.0, jnp.exp(jnp.minimum(mapped, 0.0))).astype(jnp.bfloat16)


def kernel(
    n_seq, q_hbm, k_hbm, v_hbm, fw_hbm, gain_hbm, w_hbm, out_ref,
    q_buf, k_buf, v_buf, fw_buf, gain_buf, w_buf,
    vt_buf, fk_buf, intra_buf, nrm_buf, acc,
    s_buf, peer_s, p_buf, fwd, pre_out, pfx, mp_recv,
    stage, w_far, n_out, n_in,
    q_sem, kv_sem, w_sem,
    y_send, y_recv, z_send, z_recv, b_send, b_recv, mp_send, mp_recv_sem,
    wx_send, wx_recv, n_send, n_recv,
):
    grp = lax.axis_index("groups")
    me = lax.axis_index("seq")
    mp = lax.axis_index("mp")
    layer = lax.div(me, 2)
    side = lax.rem(me, 2)
    mate = (grp, me + 1 - 2 * side, mp)
    up = (grp, me + 2, mp)
    down = (grp, me - 2, mp)
    other_mp = 1 - mp
    peer = (grp, me, other_mp)
    has_down = layer > 0
    has_up = me + 2 < n_seq
    bottom = jnp.logical_not(has_down)
    top = jnp.logical_not(has_up)
    y_out = jnp.logical_or(side == 0, has_up)
    y_in = jnp.logical_or(side == 1, has_up)
    b_out = jnp.logical_or(side == 0, has_down)
    b_in = jnp.logical_or(side == 1, has_down)
    n_pairs = q_buf.shape[0]
    rows = q_buf.shape[1]
    half = rows // 2
    n_cols = acc.shape[0]
    n_kv = k_buf.shape[1] // HD
    pairs_kv = n_pairs // n_kv
    own_pairs = n_pairs // 2
    own_heads = 2 * own_pairs
    n_parts = own_heads * CUTS
    n_head = n_pairs - TAIL
    own_at = side * own_pairs
    mate_at = own_pairs - own_at

    def k_copy():
        return pltpu.make_async_copy(k_hbm, k_buf, kv_sem.at[0])

    def v_copy():
        return pltpu.make_async_copy(v_hbm, v_buf, kv_sem.at[1])

    def fw_copy():
        return pltpu.make_async_copy(fw_hbm, fw_buf, kv_sem.at[2])

    def gain_copy():
        return pltpu.make_async_copy(gain_hbm, gain_buf, kv_sem.at[3])

    def q_copy(i):
        at = pl.multiple_of(i * PAIR, PAIR)
        return pltpu.make_async_copy(q_hbm.at[:, pl.ds(at, PAIR)], q_buf.at[i], q_sem.at[i])

    def pair_of(j):
        return lax.rem(own_at + j, n_pairs)

    def w_copy(j):
        at = pl.multiple_of(pair_of(j) * PAIR, PAIR)
        to = pl.multiple_of(j * PAIR, PAIR)
        return pltpu.make_async_copy(w_hbm.at[pl.ds(at, PAIR), :], w_buf.at[pl.ds(to, PAIR), :], w_sem.at[j])

    def remote(src, dst, send, recv, device):
        return pltpu.make_async_remote_copy(
            src_ref=src, dst_ref=dst, send_sem=send, recv_sem=recv, device_id=device, device_id_type=MESH)

    def y_copy(k):
        return remote(s_buf.at[2 * CUTS * mate_at + k], peer_s.at[k], y_send.at[k], y_recv.at[k], mate)

    def z_copy(k):
        return remote(fwd.at[k], p_buf.at[k], z_send.at[k], z_recv.at[k], up)

    def b_copy(k):
        return remote(pre_out.at[k], pfx.at[n_parts + k], b_send.at[k], b_recv.at[k], mate)

    def mp_copy(c):
        return remote(
            acc.at[c], mp_recv.at[c],
            mp_send.at[c], mp_recv_sem.at[c], peer)

    def wx_copy(t, c):
        return remote(stage.at[t, c], w_far.at[t, c], wx_send.at[t, c], wx_recv.at[t, c], peer)

    def n_copy(t):
        return remote(n_out.at[t], n_in.at[t], n_send.at[t], n_recv.at[t], peer)

    k_copy().start()
    fw_copy().start()
    v_copy().start()

    barrier = pltpu.get_barrier_semaphore()
    pl.semaphore_signal(barrier, inc=1, device_id=mate, device_id_type=MESH)
    pl.semaphore_signal(barrier, inc=1, device_id=peer, device_id_type=MESH)

    @pl.when(has_up)
    def _():
        pl.semaphore_signal(barrier, inc=1, device_id=up, device_id_type=MESH)

    @pl.when(has_down)
    def _():
        pl.semaphore_signal(barrier, inc=1, device_id=down, device_id_type=MESH)

    gain_copy().start()

    for t in range(TAIL):
        w_copy(n_head + t).start()
    for t in range(2):
        q_copy(pair_of(t)).start()

    @pl.loop(2, n_pairs)
    def _(t):
        q_copy(pair_of(t)).start()

    @pl.loop(0, n_head)
    def _(t):
        w_copy(t).start()

    @pl.when(bottom)
    def _():
        p_buf[...] = jnp.zeros_like(p_buf)

    @pl.when(jnp.logical_not(b_in))
    def _():
        pfx[n_parts:] = jnp.zeros((n_parts, PART, HD), jnp.float32)

    k_copy().wait()
    fw_copy().wait()
    v_copy().wait()

    for g in range(n_kv):
        vt_buf[g] = v_buf[:, g * HD:(g + 1) * HD].T

    def states(i):
        kv_at = pl.multiple_of(lax.div(i, pairs_kv) * HD, HD)
        weight = jnp.concatenate([fw_buf[2 * i], fw_buf[2 * i + 1]], axis=1)
        fk = feature(jnp.dot(k_buf[:, pl.ds(kv_at, HD)], weight, preferred_element_type=jnp.float32))
        fk_buf[i] = fk
        state = jnp.dot(vt_buf[lax.div(i, pairs_kv)], fk, preferred_element_type=jnp.float32)
        for d in range(2):
            s_buf[pl.ds((2 * i + d) * CUTS, CUTS)] = state[:, d * HD:(d + 1) * HD].reshape(CUTS, PART, HD)

    @pl.loop(0, n_pairs, unroll=4)
    def _(t):
        states(lax.rem(mate_at + t, n_pairs))

    cols_step = n_cols // 4
    soon = 2

    def stage_cols(u):
        for d in range(cols_step):
            c = u * cols_step + d
            cols = pl.ds(pl.multiple_of(c * COLS, COLS), COLS)
            for t in range(TAIL):
                stage[t, c] = w_buf[pl.ds((n_head + t) * PAIR, PAIR), cols].astype(jnp.float32)

    def send_cols(u):
        for d in range(cols_step):
            for t in range(TAIL):
                wx_copy(t, u * cols_step + d).start()

    for t in range(TAIL):
        w_copy(n_head + t).wait()

    @pl.loop(0, soon)
    def _(u):
        stage_cols(u)

    pl.semaphore_wait(barrier, 2 + has_up.astype(jnp.int32) + has_down.astype(jnp.int32))

    @pl.when(y_out)
    def _():
        @pl.loop(0, n_parts)
        def _(k):
            y_copy(k).start()

    @pl.loop(0, soon)
    def _(u):
        send_cols(u)

    gain_copy().wait()

    def intra(i):
        zero = jnp.zeros((HD, HD), jnp.bfloat16)
        weight = jnp.concatenate(
            [jnp.concatenate([fw_buf[2 * i], zero], axis=1),
             jnp.concatenate([zero, fw_buf[2 * i + 1]], axis=1)], axis=0)
        fq = feature(jnp.dot(q_buf[i], weight, preferred_element_type=jnp.float32))
        q_buf[i] = fq
        kv_at = pl.multiple_of(lax.div(i, pairs_kv) * HD, HD)
        values = v_buf[:, pl.ds(kv_at, HD)]
        causal = (lax.broadcasted_iota(jnp.int32, (half, half), 0)
                  >= lax.broadcasted_iota(jnp.int32, (half, half), 1))
        for j in range(2):
            lanes = slice(j * HD, (j + 1) * HD)
            fk_h = fk_buf[i, :, lanes]
            fq_h = fq[:, lanes]
            first = lax.dot_general(fq_h[:half], fk_h[:half], NT, preferred_element_type=jnp.float32)
            first = jnp.where(causal, first, 0.0).astype(jnp.bfloat16)
            intra_buf[i, :half, lanes] = jnp.dot(first, values[:half], preferred_element_type=jnp.float32)
            left = lax.dot_general(fq_h[half:], fk_h[:half], NT, preferred_element_type=jnp.float32)
            right = lax.dot_general(fq_h[half:], fk_h[half:], NT, preferred_element_type=jnp.float32)
            right = jnp.where(causal, right, 0.0)
            low = jnp.concatenate([left.astype(jnp.bfloat16), right.astype(jnp.bfloat16)], axis=1)
            intra_buf[i, half:, lanes] = jnp.dot(low, values, preferred_element_type=jnp.float32)

    def serve(k):
        @pl.when(y_in)
        def _():
            y_copy(k).wait_recv()

        @pl.when(has_down)
        def _():
            z_copy(k).wait_recv()

        @pl.when(has_up)
        def _():
            fwd[k] = p_buf[k] + s_buf[2 * CUTS * own_at + k] + peer_s[k]
            z_copy(k).start()

        @pl.when(b_out)
        def _():
            pre_out[k] = p_buf[k] + jnp.where(side == 0, s_buf[2 * CUTS * own_at + k], 0.0)
            b_copy(k).start()

        pfx[k] = p_buf[k] + jnp.where(side == 1, peer_s[k], 0.0)

    def serve_head(h):
        for d in range(CUTS):
            serve(h * CUTS + d)

    second = layer == 1
    first_due = jnp.where(bottom, 3, jnp.where(second, 7, n_pairs))
    served = n_pairs - first_due
    @pl.loop(0, n_pairs)
    def _(u):
        @pl.when(u >= first_due)
        def _():
            serve_head(u - first_due)

        i = pair_of(u)
        q_copy(i).wait()
        intra(i)
        acc[u] = jnp.zeros((half, COLS), jnp.float32)

    @pl.when(layer >= 2)
    def _():
        @pl.loop(soon, 4)
        def _(u):
            stage_cols(u)
            send_cols(u)

    theirs = pl.ds(pl.multiple_of(other_mp * half, half), half)
    mine = pl.ds(pl.multiple_of(mp * half, half), half)

    def normed(j, span):
        i = pair_of(j)
        parts = []
        for d in range(2):
            lanes = slice(d * HD, (d + 1) * HD)
            prefix = pfx[pl.ds((2 * j + d) * CUTS, CUTS)].reshape(HD, HD)
            high = prefix.astype(jnp.bfloat16)
            low = (prefix - high.astype(jnp.float32)).astype(jnp.bfloat16)
            fq_h = q_buf[i, span, lanes]
            inter = lax.dot_general(
                jnp.concatenate([fq_h, fq_h], axis=1),
                jnp.concatenate([high, low], axis=1),
                NT, preferred_element_type=jnp.float32)
            attn = inter + intra_buf[i, span, lanes]
            scale = lax.rsqrt(jnp.mean(attn * attn, axis=-1, keepdims=True) + 1e-06)
            gain = gain_buf[pl.ds(2 * i + d, 1), :]
            parts.append((attn * scale * gain).astype(jnp.bfloat16))
        return jnp.concatenate(parts, axis=1)

    def mate_prefix(j):
        for d in range(2 * CUTS):
            b_copy((2 * j - own_heads) * CUTS + d).wait_recv()

    def attend(j):
        @pl.when(jnp.logical_and(j >= own_pairs, b_in))
        def _():
            mate_prefix(j)

        w_copy(j).wait()
        at = pl.multiple_of(j * PAIR, PAIR)
        sent = normed(j, theirs)
        for c in range(n_cols):
            acc[c] += jnp.dot(
                sent, w_buf[pl.ds(at, PAIR), c * COLS:(c + 1) * COLS], preferred_element_type=jnp.float32)
        nrm_buf[:, pl.ds(at, PAIR)] = normed(j, mine)

    def attend_last(t):
        j = n_head + t

        @pl.when(b_in)
        def _():
            mate_prefix(j)

        n_out[t] = normed(j, theirs).astype(jnp.float32)
        n_copy(t).start()
        nrm_buf[:, j * PAIR:(j + 1) * PAIR] = normed(j, mine)

    @pl.loop(0, own_heads + own_pairs)
    def _(t):
        @pl.when(jnp.logical_and(t < own_heads, t >= served))
        def _():
            serve_head(t)

        @pl.when(jnp.logical_and(layer < 2, jnp.logical_and(t >= 2, t < 6 - soon)))
        def _():
            stage_cols(t - 2 + soon)
            send_cols(t - 2 + soon)

        odd = lax.rem(t, 2) == 1
        turn = lax.div(t, 2)
        inside = t < own_heads
        mid = own_heads // 2
        j_low = jnp.where(inside, turn, t - own_pairs)
        go_low = jnp.logical_or(odd, t >= own_heads)
        j_top = jnp.where(inside, jnp.where(odd, turn, own_pairs + turn - lax.div(mid, 2)), t - own_pairs + lax.div(mid, 2))
        go_top = jnp.logical_or(odd, t >= mid)
        j_bottom = t - (own_heads - 2)
        j = jnp.where(bottom, j_bottom, jnp.where(top, j_top, j_low))
        go = jnp.where(bottom, j_bottom >= 0, jnp.where(top, go_top, go_low))
        go = jnp.logical_and(go, j < n_head)

        @pl.when(go)
        def _():
            attend(j)

    @pl.loop(0, AHEAD)
    def _(c):
        mp_copy(c).start()

    @pl.loop(0, n_cols)
    def _(c):
        for t in range(TAIL):
            wx_copy(t, c).wait_send()

    total = stage.at[0]
    deep = n_head * PAIR

    def own_rows(c):
        at = pl.multiple_of(c * COLS, COLS)
        total[c] = jnp.dot(nrm_buf[:, :deep], w_buf[:deep, pl.ds(at, COLS)], preferred_element_type=jnp.float32)

    gap = n_cols // TAIL
    for t in range(TAIL):
        attend_last(t)

        if t == TAIL - 1:
            @pl.loop(AHEAD + MORE, n_cols)
            def _(c):
                mp_copy(c).start()

        @pl.loop(t * gap, (t + 1) * gap)
        def _(c):
            if t < TAIL - 1:
                @pl.when(c < MORE)
                def _():
                    mp_copy(AHEAD + c).start()

            own_rows(c)

    for t in range(TAIL):
        n_copy(t).wait_recv()

    @pl.loop(0, n_cols)
    def _(c):
        for t in range(TAIL):
            wx_copy(t, c).wait_recv()

    far = jnp.concatenate([n_in[t] for t in range(TAIL)], axis=1).astype(jnp.bfloat16)
    last = jnp.concatenate([nrm_buf[:, deep:], far], axis=1)

    @pl.loop(0, n_cols, unroll=2)
    def _(c):
        at = pl.multiple_of(c * COLS, COLS)
        weight = jnp.concatenate(
            [w_buf[deep:, pl.ds(at, COLS)]] + [w_far[t, c].astype(jnp.bfloat16) for t in range(TAIL)], axis=0)
        total[c] += jnp.dot(last, weight, preferred_element_type=jnp.float32)

    @pl.loop(0, n_cols)
    def _(c):
        mp_copy(c).wait_recv()
        at = pl.multiple_of(c * COLS, COLS)
        out_ref[:, pl.ds(at, COLS)] = (total[c] + mp_recv[c]).astype(jnp.bfloat16)

    for t in range(TAIL):
        n_copy(t).wait_send()

    @pl.loop(0, n_parts)
    def _(k):
        @pl.when(y_out)
        def _():
            y_copy(k).wait_send()

        @pl.when(b_out)
        def _():
            b_copy(k).wait_send()

        @pl.when(has_up)
        def _():
            z_copy(k).wait_send()

    @pl.loop(0, n_cols)
    def _(c):
        mp_copy(c).wait_send()


def body(n_seq, queries, keys, values, feat_weight, head_gain, out_weight):
    rows, feats = queries.shape
    heads = feat_weight.shape[0]
    n_pairs = heads // 2
    n_parts = n_pairs * CUTS
    dout = out_weight.shape[1]
    n_cols = dout // COLS
    half = rows // 2
    bf, f32 = jnp.bfloat16, jnp.float32
    gain = head_gain.reshape(heads, HD)
    dma = pltpu.SemaphoreType.DMA
    return pl.pallas_call(
        functools.partial(kernel, n_seq),
        out_shape=pltpu.VMEM((half, dout), bf),
        in_specs=[pl.BlockSpec(memory_space=pl.ANY)] * 6,
        out_specs=pl.BlockSpec(memory_space=pltpu.VMEM),
        scratch_shapes=[
            pltpu.VMEM((n_pairs, rows, PAIR), bf),
            pltpu.VMEM(keys.shape, bf),
            pltpu.VMEM(values.shape, bf),
            pltpu.VMEM(feat_weight.shape, bf),
            pltpu.VMEM((heads, HD), f32),
            pltpu.VMEM((feats, dout), bf),
            pltpu.VMEM((keys.shape[1] // HD, HD, rows), bf),
            pltpu.VMEM((n_pairs, rows, PAIR), bf),
            pltpu.VMEM((n_pairs, rows, PAIR), f32),
            pltpu.VMEM((half, feats), bf),
            pltpu.VMEM((n_cols, half, COLS), f32),
            pltpu.VMEM((2 * n_parts, PART, HD), f32),
            pltpu.VMEM((n_parts, PART, HD), f32),
            pltpu.VMEM((n_parts, PART, HD), f32),
            pltpu.VMEM((n_parts, PART, HD), f32),
            pltpu.VMEM((n_parts, PART, HD), f32),
            pltpu.VMEM((2 * n_parts, PART, HD), f32),
            pltpu.VMEM((n_cols, half, COLS), f32),
            pltpu.VMEM((TAIL, n_cols, PAIR, COLS), f32),
            pltpu.VMEM((TAIL, n_cols, PAIR, COLS), f32),
            pltpu.VMEM((TAIL, half, PAIR), f32),
            pltpu.VMEM((TAIL, half, PAIR), f32),
            dma((n_pairs,)), dma((4,)), dma((n_pairs,)),
            dma((n_parts,)), dma((n_parts,)), dma((n_parts,)), dma((n_parts,)),
            dma((n_parts,)), dma((n_parts,)),
            dma((n_cols,)), dma((n_cols,)),
            dma((TAIL, n_cols)), dma((TAIL, n_cols)), dma((TAIL,)), dma((TAIL,)),
        ],
        compiler_params=pltpu.CompilerParams(
            collective_id=0, has_side_effects=True, vmem_limit_bytes=60 * 1024 * 1024),
        cost_estimate=pl.CostEstimate(
            flops=2 * rows * feats * dout, bytes_accessed=feats * dout * 2, transcendentals=0),
    )(queries, keys, values, feat_weight, gain, out_weight)


def solution(mesh):
    return jax.shard_map(
        functools.partial(body, mesh.shape["seq"]),
        mesh=mesh,
        in_specs=(
            P(("groups", "seq"), "mp"),
            P(("groups", "seq"), "mp"),
            P(("groups", "seq"), "mp"),
            P("mp", None, None),
            P("mp"),
            P("mp", None),
        ),
        out_specs=P(("groups", "seq", "mp"), None),
        check_vma=False,
    )
```

time: 42.8 us -> 41.2 us (0.963)
  Pallas kernels: 41 us -> 39.7 us
    pallas_call x1, Pallas kernels: 41 us -> 39.7 us  [body(): pl.pallas_call(functools.partial(kernel, n_seq), out_shape=pltpu.VMEM((ha...]
where the time goes in v1:
time: 41.2 us; the launch traced here: 41 us
  Pallas kernels  39.7 us (96%)
  local copies, waits for them, and re-layouts  1.32 us (3%)
    pallas_call x1, Pallas kernels, body(): pl.pallas_call(functools.partial(kernel, n_seq), out_shape=pltpu.VMEM((ha...  39.7 us
    unnamed x1, local copies, waits for them, and re-layouts  1.32 us

profile of v1, /device:TPU:26, one launch (start us, length us, event | category | flops | bytes accessed | tf_op | source)
XLA Modules:
  0.0 41.0 jit_solution(11542075153753019517)
XLA Ops:
  0.0 39.7 %shard_map.64 = bf16[256,4096]{1,0:T(8,128)(2,1)S(1)} custom-call(bf16[512,2048]{1,0:T(8,128)(2,1)} %q_hbm.1, bf16[512,256]{1,0:T(8,128)(2,1)} %k_hbm.1, bf16[512,256]{1,0:T(8,128)(2,1)} %v_hbm.1, bf16[16,128,128]{2,1,0:T(8,128)(2,1)} %fw_hbm.1, f32[16,128]{1,0:T(8,128)} %bitcast.1, bf16[2048,4096]{1,0:T(8,128)(2,1)} %w_hbm.1), custom_call_target="tpu_custom_call" | custom-call | flops 8589934592 | bytes 16777216 | tf_op jit(solution)/shard_map/pallas_call | solution.py:449
  39.7 1.3 %copy.8 = bf16[256,4096]{1,0:T(8,128)(2,1)} copy(bf16[256,4096]{1,0:T(8,128)(2,1)S(1)} %shard_map.64) | data formatting | bytes 4194304

commit v2 on v1

--- a/solution.py
+++ b/solution.py
@@ -375,18 +375,18 @@
     for t in range(TAIL):
         attend_last(t)
 
+        if t < TAIL - 1:
+            @pl.loop(AHEAD, AHEAD + MORE)
+            def _(c):
+                mp_copy(c).start()
+
         if t == TAIL - 1:
             @pl.loop(AHEAD + MORE, n_cols)
             def _(c):
                 mp_copy(c).start()
 
-        @pl.loop(t * gap, (t + 1) * gap)
+        @pl.loop(t * gap, (t + 1) * gap, unroll=4)
         def _(c):
-            if t < TAIL - 1:
-                @pl.when(c < MORE)
-                def _():
-                    mp_copy(AHEAD + c).start()
-
             own_rows(c)
 
     for t in range(TAIL):
@@ -400,14 +400,14 @@
     far = jnp.concatenate([n_in[t] for t in range(TAIL)], axis=1).astype(jnp.bfloat16)
     last = jnp.concatenate([nrm_buf[:, deep:], far], axis=1)
 
-    @pl.loop(0, n_cols, unroll=2)
+    @pl.loop(0, n_cols, unroll=8)
     def _(c):
         at = pl.multiple_of(c * COLS, COLS)
         weight = jnp.concatenate(
             [w_buf[deep:, pl.ds(at, COLS)]] + [w_far[t, c].astype(jnp.bfloat16) for t in range(TAIL)], axis=0)
         total[c] += jnp.dot(last, weight, preferred_element_type=jnp.float32)
 
-    @pl.loop(0, n_cols)
+    @pl.loop(0, n_cols, unroll=2)
     def _(c):
         mp_copy(c).wait_recv()
         at = pl.multiple_of(c * COLS, COLS)

time: 41.2 us -> 39.6 us (0.961)
  Pallas kernels: 39.7 us -> 37.9 us
    pallas_call x1, Pallas kernels: 39.7 us -> 37.9 us  [body(): pl.pallas_call(functools.partial(kernel, n_seq), out_shape=pltpu.VMEM((ha...]
where the time goes in v2:
time: 39.6 us; the launch traced here: 39.2 us
  Pallas kernels  37.9 us (96%)
  local copies, waits for them, and re-layouts  1.32 us (3%)
    pallas_call x1, Pallas kernels, body(): pl.pallas_call(functools.partial(kernel, n_seq), out_shape=pltpu.VMEM((ha...  37.9 us
    unnamed x1, local copies, waits for them, and re-layouts  1.32 us

profile of v2, /device:TPU:26, one launch (start us, length us, event | category | flops | bytes accessed | tf_op | source)
XLA Modules:
  0.0 39.2 jit_solution(15831684077178492618)
XLA Ops:
  0.0 37.9 %shard_map.64 = bf16[256,4096]{1,0:T(8,128)(2,1)S(1)} custom-call(bf16[512,2048]{1,0:T(8,128)(2,1)} %q_hbm.1, bf16[512,256]{1,0:T(8,128)(2,1)} %k_hbm.1, bf16[512,256]{1,0:T(8,128)(2,1)} %v_hbm.1, bf16[16,128,128]{2,1,0:T(8,128)(2,1)} %fw_hbm.1, f32[16,128]{1,0:T(8,128)} %bitcast.1, bf16[2048,4096]{1,0:T(8,128)(2,1)} %w_hbm.1), custom_call_target="tpu_custom_call" | custom-call | flops 8589934592 | bytes 16777216 | tf_op jit(solution)/shard_map/pallas_call | solution.py:449
  37.9 1.3 %copy.8 = bf16[256,4096]{1,0:T(8,128)(2,1)} copy(bf16[256,4096]{1,0:T(8,128)(2,1)S(1)} %shard_map.64) | data formatting | bytes 4194304

commit v3 on v2

--- a/solution.py
+++ b/solution.py
@@ -329,6 +329,14 @@
 
     @pl.loop(0, own_heads + own_pairs)
     def _(t):
+        @pl.when(t == own_heads - has_down.astype(jnp.int32))
+        def _():
+            @pl.when(y_out)
+            def _():
+                @pl.loop(0, n_parts)
+                def _(k):
+                    y_copy(k).wait_send()
+
         @pl.when(jnp.logical_and(t < own_heads, t >= served))
         def _():
             serve_head(t)
@@ -363,6 +371,7 @@
     def _(c):
         for t in range(TAIL):
             wx_copy(t, c).wait_send()
+            wx_copy(t, c).wait_recv()
 
     total = stage.at[0]
     deep = n_head * PAIR
@@ -391,11 +400,6 @@
 
     for t in range(TAIL):
         n_copy(t).wait_recv()
-
-    @pl.loop(0, n_cols)
-    def _(c):
-        for t in range(TAIL):
-            wx_copy(t, c).wait_recv()
 
     far = jnp.concatenate([n_in[t] for t in range(TAIL)], axis=1).astype(jnp.bfloat16)
     last = jnp.concatenate([nrm_buf[:, deep:], far], axis=1)
@@ -407,28 +411,24 @@
             [w_buf[deep:, pl.ds(at, COLS)]] + [w_far[t, c].astype(jnp.bfloat16) for t in range(TAIL)], axis=0)
         total[c] += jnp.dot(last, weight, preferred_element_type=jnp.float32)
 
-    @pl.loop(0, n_cols, unroll=2)
+    for t in range(TAIL):
+        n_copy(t).wait_send()
+
+    @pl.loop(0, n_parts)
+    def _(k):
+        @pl.when(b_out)
+        def _():
+            b_copy(k).wait_send()
+
+        @pl.when(has_up)
+        def _():
+            z_copy(k).wait_send()
+
+    @pl.loop(0, n_cols, unroll=4)
     def _(c):
         mp_copy(c).wait_recv()
         at = pl.multiple_of(c * COLS, COLS)
         out_ref[:, pl.ds(at, COLS)] = (total[c] + mp_recv[c]).astype(jnp.bfloat16)
-
-    for t in range(TAIL):
-        n_copy(t).wait_send()
-
-    @pl.loop(0, n_parts)
-    def _(k):
-        @pl.when(y_out)
-        def _():
-            y_copy(k).wait_send()
-
-        @pl.when(b_out)
-        def _():
-            b_copy(k).wait_send()
-
-        @pl.when(has_up)
-        def _():
-            z_copy(k).wait_send()
 
     @pl.loop(0, n_cols)
     def _(c):

time: 39.6 us -> 39.8 us (level)
  no operation moved by 1% of the time
where the time goes in v3:
time: 39.8 us; the launch traced here: 39.2 us
  Pallas kernels  37.9 us (95%)
  local copies, waits for them, and re-layouts  1.32 us (3%)
    pallas_call x1, Pallas kernels, body(): pl.pallas_call(functools.partial(kernel, n_seq), out_shape=pltpu.VMEM((ha...  37.9 us
    unnamed x1, local copies, waits for them, and re-layouts  1.32 us

profile of v3, /device:TPU:26, one launch (start us, length us, event | category | flops | bytes accessed | tf_op | source)
XLA Modules:
  0.0 39.2 jit_solution(2102039182048016222)
XLA Ops:
  0.0 37.9 %shard_map.64 = bf16[256,4096]{1,0:T(8,128)(2,1)S(1)} custom-call(bf16[512,2048]{1,0:T(8,128)(2,1)} %q_hbm.1, bf16[512,256]{1,0:T(8,128)(2,1)} %k_hbm.1, bf16[512,256]{1,0:T(8,128)(2,1)} %v_hbm.1, bf16[16,128,128]{2,1,0:T(8,128)(2,1)} %fw_hbm.1, f32[16,128]{1,0:T(8,128)} %bitcast.1, bf16[2048,4096]{1,0:T(8,128)(2,1)} %w_hbm.1), custom_call_target="tpu_custom_call" | custom-call | flops 8589934592 | bytes 16777216 | tf_op jit(solution)/shard_map/pallas_call | solution.py:449
  37.9 1.3 %copy.8 = bf16[256,4096]{1,0:T(8,128)(2,1)} copy(bf16[256,4096]{1,0:T(8,128)(2,1)S(1)} %shard_map.64) | data formatting | bytes 4194304

commit v4 on v3

--- a/solution.py
+++ b/solution.py
@@ -167,7 +167,7 @@
         for d in range(2):
             s_buf[pl.ds((2 * i + d) * CUTS, CUTS)] = state[:, d * HD:(d + 1) * HD].reshape(CUTS, PART, HD)
 
-    @pl.loop(0, n_pairs, unroll=4)
+    @pl.loop(0, n_pairs, unroll=8)
     def _(t):
         states(lax.rem(mate_at + t, n_pairs))
 

time: 39.8 us -> 39.5 us (level)
  no operation moved by 1% of the time
where the time goes in v4:
time: 39.5 us; the launch traced here: 39 us
  Pallas kernels  37.6 us (95%)
  local copies, waits for them, and re-layouts  1.32 us (3%)
    pallas_call x1, Pallas kernels, body(): pl.pallas_call(functools.partial(kernel, n_seq), out_shape=pltpu.VMEM((ha...  37.6 us
    unnamed x1, local copies, waits for them, and re-layouts  1.32 us

profile of v4, /device:TPU:26, one launch (start us, length us, event | category | flops | bytes accessed | tf_op | source)
XLA Modules:
  0.0 39.0 jit_solution(6495145437434086931)
XLA Ops:
  0.0 37.6 %shard_map.64 = bf16[256,4096]{1,0:T(8,128)(2,1)S(1)} custom-call(bf16[512,2048]{1,0:T(8,128)(2,1)} %q_hbm.1, bf16[512,256]{1,0:T(8,128)(2,1)} %k_hbm.1, bf16[512,256]{1,0:T(8,128)(2,1)} %v_hbm.1, bf16[16,128,128]{2,1,0:T(8,128)(2,1)} %fw_hbm.1, f32[16,128]{1,0:T(8,128)} %bitcast.1, bf16[2048,4096]{1,0:T(8,128)(2,1)} %w_hbm.1), custom_call_target="tpu_custom_call" | custom-call | flops 8589934592 | bytes 16777216 | tf_op jit(solution)/shard_map/pallas_call | solution.py:449
  37.6 1.3 %copy.8 = bf16[256,4096]{1,0:T(8,128)(2,1)} copy(bf16[256,4096]{1,0:T(8,128)(2,1)S(1)} %shard_map.64) | data formatting | bytes 4194304
